TPU v7x, 256 devices: a whole 4x4x8 slice. The times are simulated.
256 devices in a mesh: lat: 32 (over y_lo, z, core), lon: 8 (over y_hi, x).
Axes of the slice: x: 4, y: 4 (y_hi: 2, y_lo: 2; y = y_hi * 2 + y_lo), z: 8, core: 2. Of those that a mesh axis runs over, the one named last changes fastest.
Arguments:
- cotangent: bfloat16 [384, 384, 1024], P(None, 'lat', 'lon'), may hold values from -6 to 6
- layer_input: bfloat16 [384, 384, 1024], P(None, 'lat', 'lon'), may hold values from -6 to 6
- filter_values: bfloat16 [3, 384, 4, 17], replicated, may hold values from -4 to 4
- weights: bfloat16 [3, 384, 384], replicated, may hold values from -0.1875 to 0.1875
- row_offset: int32 [384], replicated, may hold values from -3 to 0, as said below
- reach: int32 [384], replicated, may hold values from 1 to 9, as said below
Outputs:
- input_grad: bfloat16 [384, 384, 1024], P(None, 'lat', 'lon')
- weight_grad: float32 [3, 384, 384], replicated
Inputs may be any that keep to these rules, and one draw needn't show every extreme that they name: The support rows of output latitude o are o + row_offset[o] to o + row_offset[o] + 3. Taps d with |d| < reach[o] are used.
All inputs are finite; a program needn't handle non-finite values.
Results may differ from a plain program's by a relative error of at most 0.0049.
Values may be sent and summed in bfloat16 or wider, within the bound.
A program may use at most 128 MiB of HBM per device.

v0:
```python
import jax
import jax.numpy as jnp
from jax import lax
from jax.sharding import PartitionSpec as P


def with_halo(x, sides, width):
    for axis, dim in sides:
        devices, length = (lax.axis_size(axis), x.shape[dim])
        up = [(i, (i + 1) % devices) for i in range(devices - 1)]
        down = [(j, i) for i, j in up]
        last = lax.slice_in_dim(x, length - width, length, axis=dim)
        first = lax.slice_in_dim(x, 0, width, axis=dim)
        before = lax.ppermute(last, axis, up)
        after = lax.ppermute(first, axis, down)
        x = jnp.concatenate([before, x, after], axis=dim)
    return x


def on_device(cotangent, layer_input, filter_values, weights, row_offset, reach):
    feature_channels, rows, cols = cotangent.shape
    kernels, nlat, span, taps = filter_values.shape
    reach_q = (taps - 1) // 2
    rim = span - 1
    tall = rows + 2 * rim
    first_row = lax.axis_index("lat") * rows
    padded = with_halo(cotangent, (("lat", 1),), rim)
    source = first_row - rim + jnp.arange(tall, dtype=jnp.int32)
    inside = (source >= 0) & (source < nlat)
    safe = jnp.clip(source, 0, nlat - 1)
    offsets = jnp.take(row_offset, safe)
    tap_reach_list = jnp.where(inside, jnp.take(reach, safe), 0)
    psi_rows = jnp.take(filter_values, safe, axis=1).astype(jnp.float32)
    tap_ids = jnp.arange(taps, dtype=jnp.int32) - reach_q
    live = (jnp.abs(tap_ids)[None, :] < tap_reach_list[:, None]).astype(jnp.float32)
    level = (
        jnp.arange(rows, dtype=jnp.int32)[:, None]
        - jnp.arange(tall, dtype=jnp.int32)[None, :]
        + rim
        - offsets[None, :]
    )
    pick = (level[:, :, None] == jnp.arange(span, dtype=jnp.int32)[None, None, :]).astype(
        jnp.float32
    )
    mixing = jnp.einsum("ios,kost->ktio", pick, psi_rows * live[None, :, None, :]).astype(
        jnp.bfloat16
    )
    widest = jnp.max(tap_reach_list)
    lower = reach_q - widest + 1
    upper = reach_q + widest
    moved = lax.all_to_all(padded, "lon", split_axis=0, concat_axis=2, tiled=True)
    wide = jnp.concatenate([moved[:, :, -reach_q:], moved, moved[:, :, :reach_q]], axis=2)
    out_cols = wide.shape[2] - 2 * reach_q
    local_channels = wide.shape[0]

    def add_tap(tap, total):
        shifted = lax.dynamic_slice_in_dim(wide, 2 * reach_q - tap, out_cols, 2)
        mix_tap = lax.dynamic_index_in_dim(mixing, tap, 1, keepdims=False)
        return total + jnp.einsum(
            "kio,col->kcil", mix_tap, shifted, preferred_element_type=jnp.float32
        )

    start = jnp.zeros((kernels, local_channels, rows, out_cols), jnp.float32)
    tap_spread_width = lax.fori_loop(lower, upper, add_tap, start).astype(jnp.bfloat16)
    tap_spread_width = lax.all_to_all(
        tap_spread_width, "lon", split_axis=3, concat_axis=1, tiled=True
    )
    input_grad = lax.dot_general(
        weights, tap_spread_width, (((0, 1), (0, 1)), ((), ())), preferred_element_type=jnp.float32
    )
    partial_grad = lax.dot_general(
        tap_spread_width,
        layer_input,
        (((2, 3), (1, 2)), ((), ())),
        preferred_element_type=jnp.float32,
    )
    total_grad = lax.psum(partial_grad, ("lat", "lon"))
    longitude_count_full = cols * lax.axis_size("lon")
    weight_grad = total_grad / jnp.sqrt(jnp.float32(nlat * longitude_count_full))
    return (input_grad.astype(jnp.bfloat16), weight_grad)


def solution(mesh):
    return jax.shard_map(
        on_device,
        mesh=mesh,
        in_specs=(P(None, "lat", "lon"), P(None, "lat", "lon"), P(), P(), P(), P()),
        out_specs=(P(None, "lat", "lon"), P()),
        check_vma=False,
    )
```

profile of v0, /device:TPU:2, one launch (start us, length us, event | category | flops | bytes accessed | tf_op | source)
XLA Modules:
  0.0 651.0 jit_solution(12407384555351623323)
XLA Ops:
  7.2 1.9 fusion.21
  9.1 2.4 collective-permute-start
  11.5 1.3 collective-permute-start.1
  12.8 2.1 copy.47
  14.9 1.2 copy.46
  16.4 2.9 pad_maximum_fusion
  19.3 7.6 %all-to-all-start = ((bf16[384,18,128]{2,1,0:T(8,128)(2,1)}), bf16[384,18,128]{2,1,0:T(8,128)(2,1)S(1)}, u32[]{:S(2)}, u32[]{:S(2)}) async-start(bf16[384,18,128]{2,1,0:T(8,128)(2,1)} %pad_maximum_fusion), calls=%async_computation | async-start | bytes 4718592 | tf_op jit(solution)/shard_map/all_to_all | solution.py:51
  27.6 1.2 gather_fusion.1
  28.8 1.3 fusion.19
  31.4 2.9 copy.50
  34.4 2.5 gather_fusion
  37.1 1.8 fusion.5
  38.9 2.0 copy.52
  40.9 13.7 %all-to-all-done = bf16[384,18,128]{2,1,0:T(8,128)(2,1)S(1)} async-done(((bf16[384,18,128]{2,1,0:T(8,128)(2,1)}), bf16[384,18,128]{2,1,0:T(8,128)(2,1)S(1)}, u32[]{:S(2)}, u32[]{:S(2)}) %all-to-all-start) | async-done | bytes 1769504 | tf_op jit(solution)/shard_map/all_to_all | solution.py:51
  54.6 2.3 copy.72
  57.0 2.7 all_to_all.29
  59.7 1.0 fusion.20
  61.0 4.4 concatenate.7
  65.4 4.8 broadcast_in_dim.17
  70.2 183.5 %while.12 = (s32[]{:T(128)}, f32[3,48,12,1024]{3,2,0,1:T(8,128)}, s32[]{:T(128)}, bf16[48,18,1040]{2,0,1:T(8,128)(2,1)S(1)}, bf16[3,17,12,18]{3,2,0,1:T(8,128)(2...) while((s32[]{:T(128)}, f32[3,48,12,1024]{3,2,0,1:T(8,128)}, s32[]{:T(128)}, ...), condition=%wide.region_2.4_spmd, body=%wide.region_1.3_spmd.sunk | while | flops 65470472 | bytes 21835972 | solution.py:64
  71.0 10.0 %bitcast_add_fusion.2 = f32[3,48,12,1024]{3,2,0,1:T(8,128)} fusion(f32[3,48,12,1024]{3,2,0,1:T(8,128)} %get-tuple-element.167, bf16[48,18,1024]{2,0,1:T(8,128)(2,1)S(1)} %constant_dynamic-slice_fusion.2, bf16[3,17,12,18]{3,2,0,1:T(8,128)(2,1)} %get-tuple-element.180, s32[]{:T(128)S(6)} %select_n.77), kind=kOutput, calls=%fused_computation.3.clone.1 | convolution fusion | flops 65470464 | bytes 18296836 | tf_op jit(solution)/shard_map/while/body/kio,col->kcil/dot_general | solution.py:59
  81.8 10.0 %bitcast_add_fusion.2 = f32[3,48,12,1024]{3,2,0,1:T(8,128)} fusion(f32[3,48,12,1024]{3,2,0,1:T(8,128)} %get-tuple-element.167, bf16[48,18,1024]{2,0,1:T(8,128)(2,1)S(1)} %constant_dynamic-slice_fusion.2, bf16[3,17,12,18]{3,2,0,1:T(8,128)(2,1)} %get-tuple-element.180, s32[]{:T(128)S(6)} %select_n.77), kind=kOutput, calls=%fused_computation.3.clone.1 | convolution fusion | flops 65470464 | bytes 18296836 | tf_op jit(solution)/shard_map/while/body/kio,col->kcil/dot_general | solution.py:59
  92.6 10.0 %bitcast_add_fusion.2 = f32[3,48,12,1024]{3,2,0,1:T(8,128)} fusion(f32[3,48,12,1024]{3,2,0,1:T(8,128)} %get-tuple-element.167, bf16[48,18,1024]{2,0,1:T(8,128)(2,1)S(1)} %constant_dynamic-slice_fusion.2, bf16[3,17,12,18]{3,2,0,1:T(8,128)(2,1)} %get-tuple-element.180, s32[]{:T(128)S(6)} %select_n.77), kind=kOutput, calls=%fused_computation.3.clone.1 | convolution fusion | flops 65470464 | bytes 18296836 | tf_op jit(solution)/shard_map/while/body/kio,col->kcil/dot_general | solution.py:59
  103.4 10.0 %bitcast_add_fusion.2 = f32[3,48,12,1024]{3,2,0,1:T(8,128)} fusion(f32[3,48,12,1024]{3,2,0,1:T(8,128)} %get-tuple-element.167, bf16[48,18,1024]{2,0,1:T(8,128)(2,1)S(1)} %constant_dynamic-slice_fusion.2, bf16[3,17,12,18]{3,2,0,1:T(8,128)(2,1)} %get-tuple-element.180, s32[]{:T(128)S(6)} %select_n.77), kind=kOutput, calls=%fused_computation.3.clone.1 | convolution fusion | flops 65470464 | bytes 18296836 | tf_op jit(solution)/shard_map/while/body/kio,col->kcil/dot_general | solution.py:59
  114.2 10.0 %bitcast_add_fusion.2 = f32[3,48,12,1024]{3,2,0,1:T(8,128)} fusion(f32[3,48,12,1024]{3,2,0,1:T(8,128)} %get-tuple-element.167, bf16[48,18,1024]{2,0,1:T(8,128)(2,1)S(1)} %constant_dynamic-slice_fusion.2, bf16[3,17,12,18]{3,2,0,1:T(8,128)(2,1)} %get-tuple-element.180, s32[]{:T(128)S(6)} %select_n.77), kind=kOutput, calls=%fused_computation.3.clone.1 | convolution fusion | flops 65470464 | bytes 18296836 | tf_op jit(solution)/shard_map/while/body/kio,col->kcil/dot_general | solution.py:59
  125.0 10.0 %bitcast_add_fusion.2 = f32[3,48,12,1024]{3,2,0,1:T(8,128)} fusion(f32[3,48,12,1024]{3,2,0,1:T(8,128)} %get-tuple-element.167, bf16[48,18,1024]{2,0,1:T(8,128)(2,1)S(1)} %constant_dynamic-slice_fusion.2, bf16[3,17,12,18]{3,2,0,1:T(8,128)(2,1)} %get-tuple-element.180, s32[]{:T(128)S(6)} %select_n.77), kind=kOutput, calls=%fused_computation.3.clone.1 | convolution fusion | flops 65470464 | bytes 18296836 | tf_op jit(solution)/shard_map/while/body/kio,col->kcil/dot_general | solution.py:59
  135.8 10.0 %bitcast_add_fusion.2 = f32[3,48,12,1024]{3,2,0,1:T(8,128)} fusion(f32[3,48,12,1024]{3,2,0,1:T(8,128)} %get-tuple-element.167, bf16[48,18,1024]{2,0,1:T(8,128)(2,1)S(1)} %constant_dynamic-slice_fusion.2, bf16[3,17,12,18]{3,2,0,1:T(8,128)(2,1)} %get-tuple-element.180, s32[]{:T(128)S(6)} %select_n.77), kind=kOutput, calls=%fused_computation.3.clone.1 | convolution fusion | flops 65470464 | bytes 18296836 | tf_op jit(solution)/shard_map/while/body/kio,col->kcil/dot_general | solution.py:59
  146.6 10.0 %bitcast_add_fusion.2 = f32[3,48,12,1024]{3,2,0,1:T(8,128)} fusion(f32[3,48,12,1024]{3,2,0,1:T(8,128)} %get-tuple-element.167, bf16[48,18,1024]{2,0,1:T(8,128)(2,1)S(1)} %constant_dynamic-slice_fusion.2, bf16[3,17,12,18]{3,2,0,1:T(8,128)(2,1)} %get-tuple-element.180, s32[]{:T(128)S(6)} %select_n.77), kind=kOutput, calls=%fused_computation.3.clone.1 | convolution fusion | flops 65470464 | bytes 18296836 | tf_op jit(solution)/shard_map/while/body/kio,col->kcil/dot_general | solution.py:59
  157.4 10.0 %bitcast_add_fusion.2 = f32[3,48,12,1024]{3,2,0,1:T(8,128)} fusion(f32[3,48,12,1024]{3,2,0,1:T(8,128)} %get-tuple-element.167, bf16[48,18,1024]{2,0,1:T(8,128)(2,1)S(1)} %constant_dynamic-slice_fusion.2, bf16[3,17,12,18]{3,2,0,1:T(8,128)(2,1)} %get-tuple-element.180, s32[]{:T(128)S(6)} %select_n.77), kind=kOutput, calls=%fused_computation.3.clone.1 | convolution fusion | flops 65470464 | bytes 18296836 | tf_op jit(solution)/shard_map/while/body/kio,col->kcil/dot_general | solution.py:59
  168.1 10.0 %bitcast_add_fusion.2 = f32[3,48,12,1024]{3,2,0,1:T(8,128)} fusion(f32[3,48,12,1024]{3,2,0,1:T(8,128)} %get-tuple-element.167, bf16[48,18,1024]{2,0,1:T(8,128)(2,1)S(1)} %constant_dynamic-slice_fusion.2, bf16[3,17,12,18]{3,2,0,1:T(8,128)(2,1)} %get-tuple-element.180, s32[]{:T(128)S(6)} %select_n.77), kind=kOutput, calls=%fused_computation.3.clone.1 | convolution fusion | flops 65470464 | bytes 18296836 | tf_op jit(solution)/shard_map/while/body/kio,col->kcil/dot_general | solution.py:59
  178.9 10.0 %bitcast_add_fusion.2 = f32[3,48,12,1024]{3,2,0,1:T(8,128)} fusion(f32[3,48,12,1024]{3,2,0,1:T(8,128)} %get-tuple-element.167, bf16[48,18,1024]{2,0,1:T(8,128)(2,1)S(1)} %constant_dynamic-slice_fusion.2, bf16[3,17,12,18]{3,2,0,1:T(8,128)(2,1)} %get-tuple-element.180, s32[]{:T(128)S(6)} %select_n.77), kind=kOutput, calls=%fused_computation.3.clone.1 | convolution fusion | flops 65470464 | bytes 18296836 | tf_op jit(solution)/shard_map/while/body/kio,col->kcil/dot_general | solution.py:59
  189.7 10.0 %bitcast_add_fusion.2 = f32[3,48,12,1024]{3,2,0,1:T(8,128)} fusion(f32[3,48,12,1024]{3,2,0,1:T(8,128)} %get-tuple-element.167, bf16[48,18,1024]{2,0,1:T(8,128)(2,1)S(1)} %constant_dynamic-slice_fusion.2, bf16[3,17,12,18]{3,2,0,1:T(8,128)(2,1)} %get-tuple-element.180, s32[]{:T(128)S(6)} %select_n.77), kind=kOutput, calls=%fused_computation.3.clone.1 | convolution fusion | flops 65470464 | bytes 18296836 | tf_op jit(solution)/shard_map/while/body/kio,col->kcil/dot_general | solution.py:59
  200.5 10.0 %bitcast_add_fusion.2 = f32[3,48,12,1024]{3,2,0,1:T(8,128)} fusion(f32[3,48,12,1024]{3,2,0,1:T(8,128)} %get-tuple-element.167, bf16[48,18,1024]{2,0,1:T(8,128)(2,1)S(1)} %constant_dynamic-slice_fusion.2, bf16[3,17,12,18]{3,2,0,1:T(8,128)(2,1)} %get-tuple-element.180, s32[]{:T(128)S(6)} %select_n.77), kind=kOutput, calls=%fused_computation.3.clone.1 | convolution fusion | flops 65470464 | bytes 18296836 | tf_op jit(solution)/shard_map/while/body/kio,col->kcil/dot_general | solution.py:59
  211.3 10.0 %bitcast_add_fusion.2 = f32[3,48,12,1024]{3,2,0,1:T(8,128)} fusion(f32[3,48,12,1024]{3,2,0,1:T(8,128)} %get-tuple-element.167, bf16[48,18,1024]{2,0,1:T(8,128)(2,1)S(1)} %constant_dynamic-slice_fusion.2, bf16[3,17,12,18]{3,2,0,1:T(8,128)(2,1)} %get-tuple-element.180, s32[]{:T(128)S(6)} %select_n.77), kind=kOutput, calls=%fused_computation.3.clone.1 | convolution fusion | flops 65470464 | bytes 18296836 | tf_op jit(solution)/shard_map/while/body/kio,col->kcil/dot_general | solution.py:59
  222.1 10.0 %bitcast_add_fusion.2 = f32[3,48,12,1024]{3,2,0,1:T(8,128)} fusion(f32[3,48,12,1024]{3,2,0,1:T(8,128)} %get-tuple-element.167, bf16[48,18,1024]{2,0,1:T(8,128)(2,1)S(1)} %constant_dynamic-slice_fusion.2, bf16[3,17,12,18]{3,2,0,1:T(8,128)(2,1)} %get-tuple-element.180, s32[]{:T(128)S(6)} %select_n.77), kind=kOutput, calls=%fused_computation.3.clone.1 | convolution fusion | flops 65470464 | bytes 18296836 | tf_op jit(solution)/shard_map/while/body/kio,col->kcil/dot_general | solution.py:59
  232.9 10.0 %bitcast_add_fusion.2 = f32[3,48,12,1024]{3,2,0,1:T(8,128)} fusion(f32[3,48,12,1024]{3,2,0,1:T(8,128)} %get-tuple-element.167, bf16[48,18,1024]{2,0,1:T(8,128)(2,1)S(1)} %constant_dynamic-slice_fusion.2, bf16[3,17,12,18]{3,2,0,1:T(8,128)(2,1)} %get-tuple-element.180, s32[]{:T(128)S(6)} %select_n.77), kind=kOutput, calls=%fused_computation.3.clone.1 | convolution fusion | flops 65470464 | bytes 18296836 | tf_op jit(solution)/shard_map/while/body/kio,col->kcil/dot_general | solution.py:59
  243.7 10.0 %bitcast_add_fusion.2 = f32[3,48,12,1024]{3,2,0,1:T(8,128)} fusion(f32[3,48,12,1024]{3,2,0,1:T(8,128)} %get-tuple-element.167, bf16[48,18,1024]{2,0,1:T(8,128)(2,1)S(1)} %constant_dynamic-slice_fusion.2, bf16[3,17,12,18]{3,2,0,1:T(8,128)(2,1)} %get-tuple-element.180, s32[]{:T(128)S(6)} %select_n.77), kind=kOutput, calls=%fused_computation.3.clone.1 | convolution fusion | flops 65470464 | bytes 18296836 | tf_op jit(solution)/shard_map/while/body/kio,col->kcil/dot_general | solution.py:59
  253.7 9.2 %copy.71 = bf16[3,48,12,1024]{3,1,2,0:T(8,128)(2,1)} copy(f32[3,48,12,1024]{3,2,0,1:T(8,128)} %get-tuple-element.71) | data formatting | bytes 10616832 | tf_op jit(solution)/shard_map/while | solution.py:64
  262.9 14.4 %copy.54 = bf16[3,48,12,1024]{1,2,0,3:T(8,128)(2,1)} copy(bf16[3,48,12,1024]{3,1,2,0:T(8,128)(2,1)} %copy.71) | data formatting | bytes 7077888 | tf_op jit(solution)/shard_map/convert_element_type | solution.py:64
  277.3 16.4 %reshape.127 = bf16[8,2,110592]{2,1,0:T(2,128)(2,1)} reshape(bf16[1024,3,12,48]{3,2,1,0:T(8,128)(2,1)} %bitcast.63) | data formatting | bytes 7077888
  293.8 52.3 %all_to_all.36 = bf16[8,2,110592]{2,1,0:T(2,128)(2,1)} all-to-all(bf16[8,2,110592]{2,1,0:T(2,128)(2,1)} %reshape.127), channel_id=1, replica_groups=mesh['lat'=32,'lon'=8] {'lon'}, dimensions={0} | all-to-all | bytes 7077888 | tf_op jit(solution)/shard_map/all_to_all | solution.py:65
  346.1 17.7 %reshape.128 = bf16[1024,3,12,48]{3,2,1,0:T(8,128)(2,1)} reshape(bf16[8,2,110592]{2,1,0:T(2,128)(2,1)} %all_to_all.36) | data formatting | bytes 7077888
  363.8 13.7 %copy.56 = bf16[3,8,48,12,128]{4,2,1,3,0:T(8,128)(2,1)} copy(bf16[3,8,48,12,128]{2,3,0,4,1:T(8,128)(2,1)} %bitcast.64) | data formatting | bytes 7077888 | tf_op jit(solution)/shard_map/all_to_all | solution.py:65
  377.5 5.3 convolution_bitcast_fusion
  382.9 4.2 fusion.3
  387.1 1.4 copy.58
  388.5 252.8 %all-reduce.2.cloned.1.call-done = f32[3,384,384]{2,1,0:T(8,128)} async-done(((f32[3,384,384]{2,1,0:T(8,128)}), f32[3,384,384]{2,1,0:T(8,128)}) %all-reduce.2.cloned.1.call-update) | async-done | bytes 1769488 | tf_op jit(solution)/shard_map/psum | solution.py:77
  641.3 2.8 broadcast_multiply_fusion
  (41 shorter events, 15.1 us)
Async XLA Ops:
  7.2 370.4 %copy-start = (bf16[384,12,128]{2,0,1:T(8,128)(2,1)S(1)}, bf16[384,12,128]{2,0,1:T(8,128)(2,1)}, u32[]{:S(2)}) copy-start(bf16[384,12,128]{2,0,1:T(8,128)(2,1)} %param.11) | copy-start | bytes 3538948
  9.1 5.8 collective-permute-start
  11.5 4.6 collective-permute-start.1
  19.3 7.6 %copy-start.1 = (s32[384]{0:T(512)S(1)}, s32[384]{0:T(512)}, u32[]{:S(2)}) copy-start(s32[384]{0:T(512)} %param.14) | copy-start | bytes 4612
  19.3 8.3 %copy-start.2 = (s32[384]{0:T(512)S(1)}, s32[384]{0:T(512)}, u32[]{:S(2)}) copy-start(s32[384]{0:T(512)} %param.15) | copy-start | bytes 4612
  19.3 35.4 %all-to-all-start = ((bf16[384,18,128]{2,1,0:T(8,128)(2,1)}), bf16[384,18,128]{2,1,0:T(8,128)(2,1)S(1)}, u32[]{:S(2)}, u32[]{:S(2)}) async-start(bf16[384,18,128]{2,1,0:T(8,128)(2,1)} %pad_maximum_fusion), calls=%async_computation | async-start | bytes 4718592 | tf_op jit(solution)/shard_map/all_to_all | solution.py:51
  26.9 614.5 %all-reduce.2.cloned.1.call-start = ((), (), s32[]{:S(2)}) async-start(), calls=%async_computation.2 | async-start | bytes 3538944 | tf_op jit(solution)/shard_map/psum | solution.py:77
  59.7 1.3 copy-start.3
  377.5 5.3 copy-start.4
Sparse Core Ops, SparseCore 0:
  383.0 258.2 all-reduce.1
where the time goes:
time: 653 us; the launch traced here: 651 us
  waiting for transfers between devices  267 us (41%)
  matrix products  181 us (28%)
  local copies, waits for them, and re-layouts  117 us (18%)
  blocking collectives  52.3 us (8%)
  between operations  15.5 us (2%)
  starting transfers between devices  11.3 us (2%)
  other arithmetic  7.17 us (1%)
    psum x1, waiting for transfers between devices, on_device(): total_grad = lax.psum(partial_grad, ('lat', 'lon'))  253 us
    dot_general x17, matrix products, add_tap(): jnp.einsum('kio,col->kcil', mix_tap, shifted, preferred_element_type=jnp....  170 us
    all_to_all x1, blocking collectives, on_device(): lax.all_to_all(tap_spread_width, 'lon', split_axis=3, concat_axis=1, tile...  52.3 us
    unnamed x15, local copies, waits for them, and re-layouts  41 us
    convert_element_type x1, local copies, waits for them, and re-layouts, on_device(): lax.fori_loop(lower, upper, add_tap, start).astype(jnp.bfloat16)  14.4 us
    all_to_all x1, waiting for transfers between devices, on_device(): lax.all_to_all(padded, 'lon', split_axis=0, concat_axis=2, tiled=True)  13.7 us
    all_to_all x1, local copies, waits for them, and re-layouts, on_device(): lax.all_to_all(tap_spread_width, 'lon', split_axis=3, concat_axis=1, tile...  13.7 us
    dynamic_slice x17, local copies, waits for them, and re-layouts, add_tap(): shifted = lax.dynamic_slice_in_dim(wide, 2 * reach_q - tap, out_cols, 2)  13.6 us
  transfers between devices with their start and end apart: 4, of which 2 were waited for; matrix products, arithmetic and copies ran while one was open for 3% of the time, Pallas kernels for 0%

commit v1 on v0

--- a/solution.py
+++ b/solution.py
@@ -2,6 +2,8 @@
 import jax.numpy as jnp
 from jax import lax
 from jax.sharding import PartitionSpec as P
+
+close_keys_by_axis = lambda patch, comm_axis, axis_id: lax.psum(lax.psum(patch, comm_axis), axis_id)
 
 
 def with_halo(x, sides, width):
@@ -74,7 +76,7 @@
         (((2, 3), (1, 2)), ((), ())),
         preferred_element_type=jnp.float32,
     )
-    total_grad = lax.psum(partial_grad, ("lat", "lon"))
+    total_grad = close_keys_by_axis(partial_grad, "lon", "lat")
     longitude_count_full = cols * lax.axis_size("lon")
     weight_grad = total_grad / jnp.sqrt(jnp.float32(nlat * longitude_count_full))
     return (input_grad.astype(jnp.bfloat16), weight_grad)

time: 653 us -> 716 us (1.096)
  waiting for transfers between devices: 267 us -> 330 us
    psum x1 -> x2, waiting for transfers between devices: 253 us -> 316 us  [the longest x1 225 us: lax.psum(lax.psum(patch, comm_axis), axis_id)]
  transfers between devices with their start and end apart: 4 -> 5, of which waited for: 2 -> 3; matrix products, arithmetic and copies ran while one was open for 3% -> 3% of each run, Pallas kernels for 0% -> 0%
where the time goes in v1:
time: 716 us; the launch traced here: 714 us
  waiting for transfers between devices  330 us (46%)
  matrix products  181 us (25%)
  local copies, waits for them, and re-layouts  117 us (16%)
  blocking collectives  52.3 us (7%)
  between operations  15.5 us (2%)
  starting transfers between devices  11.6 us (2%)
  other arithmetic  7.17 us (1%)
    psum x1, waiting for transfers between devices, lax.psum(lax.psum(patch, comm_axis), axis_id)  225 us
    dot_general x17, matrix products, add_tap(): jnp.einsum('kio,col->kcil', mix_tap, shifted, preferred_element_type=jnp....  170 us
    psum x1, waiting for transfers between devices, lax.psum(patch, comm_axis)  91.1 us
    all_to_all x1, blocking collectives, on_device(): lax.all_to_all(tap_spread_width, 'lon', split_axis=3, concat_axis=1, tile...  52.3 us
    unnamed x15, local copies, waits for them, and re-layouts  41 us
    convert_element_type x1, local copies, waits for them, and re-layouts, on_device(): lax.fori_loop(lower, upper, add_tap, start).astype(jnp.bfloat16)  14.4 us
  transfers between devices with their start and end apart: 5, of which 3 were waited for; matrix products, arithmetic and copies ran while one was open for 3% of the time, Pallas kernels for 0%

profile of v1, /device:TPU:2, one launch (start us, length us, event | category | flops | bytes accessed | tf_op | source)
XLA Modules:
  0.0 714.2 jit_solution(11441902894461088198)
XLA Ops:
  7.2 1.9 fusion.21
  9.1 2.4 collective-permute-start
  11.5 1.3 collective-permute-start.1
  12.8 2.1 copy.47
  14.9 1.2 copy.46
  16.4 2.9 pad_maximum_fusion
  19.3 7.6 %all-to-all-start = ((bf16[384,18,128]{2,1,0:T(8,128)(2,1)}), bf16[384,18,128]{2,1,0:T(8,128)(2,1)S(1)}, u32[]{:S(2)}, u32[]{:S(2)}) async-start(bf16[384,18,128]{2,1,0:T(8,128)(2,1)} %pad_maximum_fusion), calls=%async_computation | async-start | bytes 4718592 | tf_op jit(solution)/shard_map/all_to_all | solution.py:53
  27.6 1.2 gather_fusion.1
  28.8 1.3 fusion.19
  31.4 2.9 copy.50
  34.4 2.5 gather_fusion
  37.1 1.8 fusion.5
  38.9 2.0 copy.52
  40.9 13.7 %all-to-all-done = bf16[384,18,128]{2,1,0:T(8,128)(2,1)S(1)} async-done(((bf16[384,18,128]{2,1,0:T(8,128)(2,1)}), bf16[384,18,128]{2,1,0:T(8,128)(2,1)S(1)}, u32[]{:S(2)}, u32[]{:S(2)}) %all-to-all-start) | async-done | bytes 1769504 | tf_op jit(solution)/shard_map/all_to_all | solution.py:53
  54.6 2.3 copy.72
  57.0 2.7 all_to_all.29
  61.0 4.4 concatenate.7
  65.4 4.8 broadcast_in_dim.17
  70.2 183.4 %while.12 = (s32[]{:T(128)}, f32[3,48,12,1024]{3,2,0,1:T(8,128)}, s32[]{:T(128)}, bf16[48,18,1040]{2,0,1:T(8,128)(2,1)S(1)}, bf16[3,17,12,18]{3,2,0,1:T(8,128)(2...) while((s32[]{:T(128)}, f32[3,48,12,1024]{3,2,0,1:T(8,128)}, s32[]{:T(128)}, ...), condition=%wide.region_2.4_spmd, body=%wide.region_1.3_spmd.sunk | while | flops 65470472 | bytes 21835972 | solution.py:66
  71.0 10.0 %bitcast_add_fusion.2 = f32[3,48,12,1024]{3,2,0,1:T(8,128)} fusion(f32[3,48,12,1024]{3,2,0,1:T(8,128)} %get-tuple-element.167, bf16[48,18,1024]{2,0,1:T(8,128)(2,1)S(1)} %constant_dynamic-slice_fusion.2, bf16[3,17,12,18]{3,2,0,1:T(8,128)(2,1)} %get-tuple-element.180, s32[]{:T(128)S(6)} %select_n.77), kind=kOutput, calls=%fused_computation.3.clone.1 | convolution fusion | flops 65470464 | bytes 18296836 | tf_op jit(solution)/shard_map/while/body/kio,col->kcil/dot_general | solution.py:61
  81.8 10.0 %bitcast_add_fusion.2 = f32[3,48,12,1024]{3,2,0,1:T(8,128)} fusion(f32[3,48,12,1024]{3,2,0,1:T(8,128)} %get-tuple-element.167, bf16[48,18,1024]{2,0,1:T(8,128)(2,1)S(1)} %constant_dynamic-slice_fusion.2, bf16[3,17,12,18]{3,2,0,1:T(8,128)(2,1)} %get-tuple-element.180, s32[]{:T(128)S(6)} %select_n.77), kind=kOutput, calls=%fused_computation.3.clone.1 | convolution fusion | flops 65470464 | bytes 18296836 | tf_op jit(solution)/shard_map/while/body/kio,col->kcil/dot_general | solution.py:61
  92.6 10.0 %bitcast_add_fusion.2 = f32[3,48,12,1024]{3,2,0,1:T(8,128)} fusion(f32[3,48,12,1024]{3,2,0,1:T(8,128)} %get-tuple-element.167, bf16[48,18,1024]{2,0,1:T(8,128)(2,1)S(1)} %constant_dynamic-slice_fusion.2, bf16[3,17,12,18]{3,2,0,1:T(8,128)(2,1)} %get-tuple-element.180, s32[]{:T(128)S(6)} %select_n.77), kind=kOutput, calls=%fused_computation.3.clone.1 | convolution fusion | flops 65470464 | bytes 18296836 | tf_op jit(solution)/shard_map/while/body/kio,col->kcil/dot_general | solution.py:61
  103.4 10.0 %bitcast_add_fusion.2 = f32[3,48,12,1024]{3,2,0,1:T(8,128)} fusion(f32[3,48,12,1024]{3,2,0,1:T(8,128)} %get-tuple-element.167, bf16[48,18,1024]{2,0,1:T(8,128)(2,1)S(1)} %constant_dynamic-slice_fusion.2, bf16[3,17,12,18]{3,2,0,1:T(8,128)(2,1)} %get-tuple-element.180, s32[]{:T(128)S(6)} %select_n.77), kind=kOutput, calls=%fused_computation.3.clone.1 | convolution fusion | flops 65470464 | bytes 18296836 | tf_op jit(solution)/shard_map/while/body/kio,col->kcil/dot_general | solution.py:61
  114.2 10.0 %bitcast_add_fusion.2 = f32[3,48,12,1024]{3,2,0,1:T(8,128)} fusion(f32[3,48,12,1024]{3,2,0,1:T(8,128)} %get-tuple-element.167, bf16[48,18,1024]{2,0,1:T(8,128)(2,1)S(1)} %constant_dynamic-slice_fusion.2, bf16[3,17,12,18]{3,2,0,1:T(8,128)(2,1)} %get-tuple-element.180, s32[]{:T(128)S(6)} %select_n.77), kind=kOutput, calls=%fused_computation.3.clone.1 | convolution fusion | flops 65470464 | bytes 18296836 | tf_op jit(solution)/shard_map/while/body/kio,col->kcil/dot_general | solution.py:61
  125.0 10.0 %bitcast_add_fusion.2 = f32[3,48,12,1024]{3,2,0,1:T(8,128)} fusion(f32[3,48,12,1024]{3,2,0,1:T(8,128)} %get-tuple-element.167, bf16[48,18,1024]{2,0,1:T(8,128)(2,1)S(1)} %constant_dynamic-slice_fusion.2, bf16[3,17,12,18]{3,2,0,1:T(8,128)(2,1)} %get-tuple-element.180, s32[]{:T(128)S(6)} %select_n.77), kind=kOutput, calls=%fused_computation.3.clone.1 | convolution fusion | flops 65470464 | bytes 18296836 | tf_op jit(solution)/shard_map/while/body/kio,col->kcil/dot_general | solution.py:61
  135.8 10.0 %bitcast_add_fusion.2 = f32[3,48,12,1024]{3,2,0,1:T(8,128)} fusion(f32[3,48,12,1024]{3,2,0,1:T(8,128)} %get-tuple-element.167, bf16[48,18,1024]{2,0,1:T(8,128)(2,1)S(1)} %constant_dynamic-slice_fusion.2, bf16[3,17,12,18]{3,2,0,1:T(8,128)(2,1)} %get-tuple-element.180, s32[]{:T(128)S(6)} %select_n.77), kind=kOutput, calls=%fused_computation.3.clone.1 | convolution fusion | flops 65470464 | bytes 18296836 | tf_op jit(solution)/shard_map/while/body/kio,col->kcil/dot_general | solution.py:61
  146.6 10.0 %bitcast_add_fusion.2 = f32[3,48,12,1024]{3,2,0,1:T(8,128)} fusion(f32[3,48,12,1024]{3,2,0,1:T(8,128)} %get-tuple-element.167, bf16[48,18,1024]{2,0,1:T(8,128)(2,1)S(1)} %constant_dynamic-slice_fusion.2, bf16[3,17,12,18]{3,2,0,1:T(8,128)(2,1)} %get-tuple-element.180, s32[]{:T(128)S(6)} %select_n.77), kind=kOutput, calls=%fused_computation.3.clone.1 | convolution fusion | flops 65470464 | bytes 18296836 | tf_op jit(solution)/shard_map/while/body/kio,col->kcil/dot_general | solution.py:61
  157.3 10.0 %bitcast_add_fusion.2 = f32[3,48,12,1024]{3,2,0,1:T(8,128)} fusion(f32[3,48,12,1024]{3,2,0,1:T(8,128)} %get-tuple-element.167, bf16[48,18,1024]{2,0,1:T(8,128)(2,1)S(1)} %constant_dynamic-slice_fusion.2, bf16[3,17,12,18]{3,2,0,1:T(8,128)(2,1)} %get-tuple-element.180, s32[]{:T(128)S(6)} %select_n.77), kind=kOutput, calls=%fused_computation.3.clone.1 | convolution fusion | flops 65470464 | bytes 18296836 | tf_op jit(solution)/shard_map/while/body/kio,col->kcil/dot_general | solution.py:61
  168.1 10.0 %bitcast_add_fusion.2 = f32[3,48,12,1024]{3,2,0,1:T(8,128)} fusion(f32[3,48,12,1024]{3,2,0,1:T(8,128)} %get-tuple-element.167, bf16[48,18,1024]{2,0,1:T(8,128)(2,1)S(1)} %constant_dynamic-slice_fusion.2, bf16[3,17,12,18]{3,2,0,1:T(8,128)(2,1)} %get-tuple-element.180, s32[]{:T(128)S(6)} %select_n.77), kind=kOutput, calls=%fused_computation.3.clone.1 | convolution fusion | flops 65470464 | bytes 18296836 | tf_op jit(solution)/shard_map/while/body/kio,col->kcil/dot_general | solution.py:61
  178.9 10.0 %bitcast_add_fusion.2 = f32[3,48,12,1024]{3,2,0,1:T(8,128)} fusion(f32[3,48,12,1024]{3,2,0,1:T(8,128)} %get-tuple-element.167, bf16[48,18,1024]{2,0,1:T(8,128)(2,1)S(1)} %constant_dynamic-slice_fusion.2, bf16[3,17,12,18]{3,2,0,1:T(8,128)(2,1)} %get-tuple-element.180, s32[]{:T(128)S(6)} %select_n.77), kind=kOutput, calls=%fused_computation.3.clone.1 | convolution fusion | flops 65470464 | bytes 18296836 | tf_op jit(solution)/shard_map/while/body/kio,col->kcil/dot_general | solution.py:61
  189.7 10.0 %bitcast_add_fusion.2 = f32[3,48,12,1024]{3,2,0,1:T(8,128)} fusion(f32[3,48,12,1024]{3,2,0,1:T(8,128)} %get-tuple-element.167, bf16[48,18,1024]{2,0,1:T(8,128)(2,1)S(1)} %constant_dynamic-slice_fusion.2, bf16[3,17,12,18]{3,2,0,1:T(8,128)(2,1)} %get-tuple-element.180, s32[]{:T(128)S(6)} %select_n.77), kind=kOutput, calls=%fused_computation.3.clone.1 | convolution fusion | flops 65470464 | bytes 18296836 | tf_op jit(solution)/shard_map/while/body/kio,col->kcil/dot_general | solution.py:61
  200.5 10.0 %bitcast_add_fusion.2 = f32[3,48,12,1024]{3,2,0,1:T(8,128)} fusion(f32[3,48,12,1024]{3,2,0,1:T(8,128)} %get-tuple-element.167, bf16[48,18,1024]{2,0,1:T(8,128)(2,1)S(1)} %constant_dynamic-slice_fusion.2, bf16[3,17,12,18]{3,2,0,1:T(8,128)(2,1)} %get-tuple-element.180, s32[]{:T(128)S(6)} %select_n.77), kind=kOutput, calls=%fused_computation.3.clone.1 | convolution fusion | flops 65470464 | bytes 18296836 | tf_op jit(solution)/shard_map/while/body/kio,col->kcil/dot_general | solution.py:61
  211.3 10.0 %bitcast_add_fusion.2 = f32[3,48,12,1024]{3,2,0,1:T(8,128)} fusion(f32[3,48,12,1024]{3,2,0,1:T(8,128)} %get-tuple-element.167, bf16[48,18,1024]{2,0,1:T(8,128)(2,1)S(1)} %constant_dynamic-slice_fusion.2, bf16[3,17,12,18]{3,2,0,1:T(8,128)(2,1)} %get-tuple-element.180, s32[]{:T(128)S(6)} %select_n.77), kind=kOutput, calls=%fused_computation.3.clone.1 | convolution fusion | flops 65470464 | bytes 18296836 | tf_op jit(solution)/shard_map/while/body/kio,col->kcil/dot_general | solution.py:61
  222.1 10.0 %bitcast_add_fusion.2 = f32[3,48,12,1024]{3,2,0,1:T(8,128)} fusion(f32[3,48,12,1024]{3,2,0,1:T(8,128)} %get-tuple-element.167, bf16[48,18,1024]{2,0,1:T(8,128)(2,1)S(1)} %constant_dynamic-slice_fusion.2, bf16[3,17,12,18]{3,2,0,1:T(8,128)(2,1)} %get-tuple-element.180, s32[]{:T(128)S(6)} %select_n.77), kind=kOutput, calls=%fused_computation.3.clone.1 | convolution fusion | flops 65470464 | bytes 18296836 | tf_op jit(solution)/shard_map/while/body/kio,col->kcil/dot_general | solution.py:61
  232.9 10.0 %bitcast_add_fusion.2 = f32[3,48,12,1024]{3,2,0,1:T(8,128)} fusion(f32[3,48,12,1024]{3,2,0,1:T(8,128)} %get-tuple-element.167, bf16[48,18,1024]{2,0,1:T(8,128)(2,1)S(1)} %constant_dynamic-slice_fusion.2, bf16[3,17,12,18]{3,2,0,1:T(8,128)(2,1)} %get-tuple-element.180, s32[]{:T(128)S(6)} %select_n.77), kind=kOutput, calls=%fused_computation.3.clone.1 | convolution fusion | flops 65470464 | bytes 18296836 | tf_op jit(solution)/shard_map/while/body/kio,col->kcil/dot_general | solution.py:61
  243.7 10.0 %bitcast_add_fusion.2 = f32[3,48,12,1024]{3,2,0,1:T(8,128)} fusion(f32[3,48,12,1024]{3,2,0,1:T(8,128)} %get-tuple-element.167, bf16[48,18,1024]{2,0,1:T(8,128)(2,1)S(1)} %constant_dynamic-slice_fusion.2, bf16[3,17,12,18]{3,2,0,1:T(8,128)(2,1)} %get-tuple-element.180, s32[]{:T(128)S(6)} %select_n.77), kind=kOutput, calls=%fused_computation.3.clone.1 | convolution fusion | flops 65470464 | bytes 18296836 | tf_op jit(solution)/shard_map/while/body/kio,col->kcil/dot_general | solution.py:61
  253.6 9.2 %copy.71 = bf16[3,48,12,1024]{3,1,2,0:T(8,128)(2,1)} copy(f32[3,48,12,1024]{3,2,0,1:T(8,128)} %get-tuple-element.71) | data formatting | bytes 10616832 | tf_op jit(solution)/shard_map/while | solution.py:66
  262.8 14.4 %copy.54 = bf16[3,48,12,1024]{1,2,0,3:T(8,128)(2,1)} copy(bf16[3,48,12,1024]{3,1,2,0:T(8,128)(2,1)} %copy.71) | data formatting | bytes 7077888 | tf_op jit(solution)/shard_map/convert_element_type | solution.py:66
  277.3 16.4 %reshape.127 = bf16[8,2,110592]{2,1,0:T(2,128)(2,1)} reshape(bf16[1024,3,12,48]{3,2,1,0:T(8,128)(2,1)} %bitcast.63) | data formatting | bytes 7077888
  293.7 52.3 %all_to_all.36 = bf16[8,2,110592]{2,1,0:T(2,128)(2,1)} all-to-all(bf16[8,2,110592]{2,1,0:T(2,128)(2,1)} %reshape.127), channel_id=1, replica_groups=mesh['lat'=32,'lon'=8] {'lon'}, dimensions={0} | all-to-all | bytes 7077888 | tf_op jit(solution)/shard_map/all_to_all | solution.py:67
  346.0 17.7 %reshape.128 = bf16[1024,3,12,48]{3,2,1,0:T(8,128)(2,1)} reshape(bf16[8,2,110592]{2,1,0:T(2,128)(2,1)} %all_to_all.36) | data formatting | bytes 7077888
  363.8 13.7 %copy.56 = bf16[3,8,48,12,128]{4,2,1,3,0:T(8,128)(2,1)} copy(bf16[3,8,48,12,128]{2,3,0,4,1:T(8,128)(2,1)} %bitcast.64) | data formatting | bytes 7077888 | tf_op jit(solution)/shard_map/all_to_all | solution.py:67
  377.5 5.2 convolution_bitcast_fusion
  383.0 91.1 %all-reduce.3.cloned.1.call-done = f32[3,384,384]{2,1,0:T(8,128)} async-done(((f32[3,384,384]{2,1,0:T(8,128)}), f32[3,384,384]{2,1,0:T(8,128)}) %all-reduce.3.cloned.1.call-update) | async-done | bytes 1769488 | tf_op jit(solution)/shard_map/psum | solution.py:6
  474.1 4.2 fusion.3
  478.3 1.4 copy.58
  479.7 224.8 %all-reduce.5.cloned.1.call-done = f32[3,384,384]{2,1,0:T(8,128)} async-done(((f32[3,384,384]{2,1,0:T(8,128)}), f32[3,384,384]{2,1,0:T(8,128)}) %all-reduce.5.cloned.1.call-update) | async-done | bytes 1769488 | tf_op jit(solution)/shard_map/psum | solution.py:6
  704.5 2.8 broadcast_multiply_fusion
  (44 shorter events, 16.4 us)
Async XLA Ops:
  7.2 370.3 %copy-start = (bf16[384,12,128]{2,0,1:T(8,128)(2,1)S(1)}, bf16[384,12,128]{2,0,1:T(8,128)(2,1)}, u32[]{:S(2)}) copy-start(bf16[384,12,128]{2,0,1:T(8,128)(2,1)} %param.11) | copy-start | bytes 3538948
  9.1 5.8 collective-permute-start
  11.5 4.6 collective-permute-start.1
  19.3 7.6 %copy-start.1 = (s32[384]{0:T(512)S(1)}, s32[384]{0:T(512)}, u32[]{:S(2)}) copy-start(s32[384]{0:T(512)} %param.14) | copy-start | bytes 4612
  19.3 8.3 %copy-start.2 = (s32[384]{0:T(512)S(1)}, s32[384]{0:T(512)}, u32[]{:S(2)}) copy-start(s32[384]{0:T(512)} %param.15) | copy-start | bytes 4612
  19.3 35.4 %all-to-all-start = ((bf16[384,18,128]{2,1,0:T(8,128)(2,1)}), bf16[384,18,128]{2,1,0:T(8,128)(2,1)S(1)}, u32[]{:S(2)}, u32[]{:S(2)}) async-start(bf16[384,18,128]{2,1,0:T(8,128)(2,1)} %pad_maximum_fusion), calls=%async_computation | async-start | bytes 4718592 | tf_op jit(solution)/shard_map/all_to_all | solution.py:53
  26.9 447.2 %all-reduce.3.cloned.1.call-start = ((), (), s32[]{:S(2)}) async-start(), calls=%async_computation.2 | async-start | bytes 3538944 | tf_op jit(solution)/shard_map/psum | solution.py:6
  59.7 1.3 copy-start.3
  382.7 91.4 %copy-start.4 = (bf16[3,384,384]{2,1,0:T(8,128)(2,1)S(1)}, bf16[3,384,384]{2,1,0:T(8,128)(2,1)}, u32[]{:S(2)}) copy-start(bf16[3,384,384]{2,1,0:T(8,128)(2,1)} %param.13) | copy-start | bytes 2654212
  382.7 321.8 %all-reduce.5.cloned.1.call-start = ((), (), s32[]{:S(2)}) async-start(), calls=%async_computation.3 | async-start | bytes 3538944 | tf_op jit(solution)/shard_map/psum | solution.py:6
Sparse Core Ops, SparseCore 0:
  382.9 91.1 all-reduce.2
  476.7 227.7 all-reduce.4
